TPU v7x, 32 devices: a whole 2x2x4 slice. The times are simulated.
32 devices in a mesh: dp: 4 (over y, x), mp: 8 (over z, core).
Axes of the slice: x: 2, y: 2, z: 4, core: 2. Of those that a mesh axis runs over, the one named last changes fastest.
Arguments:
- inputs: bfloat16 [2048, 1024], P('dp'), may hold values from -60 to 60
- norm_gain_vector: float32 [1024], replicated, may hold values from 0.5 to 1.5
- query_saved: bfloat16 [2048, 16384], P('dp', 'mp'), may hold values from -5 to 5
- key_saved: bfloat16 [2048, 16384], P('dp', 'mp'), may hold values from -2 to 2
- value_saved: bfloat16 [2048, 16384], P('dp', 'mp'), may hold values from -6 to 6
- w_query: bfloat16 [1024, 16384], P(None, 'mp'), may hold values from -0.1875 to 0.1875
- w_key: bfloat16 [1024, 16384], P(None, 'mp'), may hold values from -0.1875 to 0.1875
- w_value: bfloat16 [1024, 16384], P(None, 'mp'), may hold values from -0.1875 to 0.1875
- w_out: bfloat16 [16384, 1024], P('mp'), may hold values from -0.046875 to 0.046875
- output_gradient: bfloat16 [2048, 1024], P('dp'), may hold values from -4 to 4
Outputs:
- grad_inputs: bfloat16 [2048, 1024], P('dp')
- grad_w_query: bfloat16 [1024, 16384], P(None, 'mp')
- grad_w_key: bfloat16 [1024, 16384], P(None, 'mp')
- grad_w_value: bfloat16 [1024, 16384], P(None, 'mp')
- grad_w_out: bfloat16 [16384, 1024], P('mp')
- grad_gain: float32 [1024], replicated
All inputs are finite; a program needn't handle non-finite values.
Results may differ from a plain program's by a relative error of at most 0.034.
Values may be sent and summed in bfloat16 or wider, within the bound.
A program may use at most 128 MiB of HBM per device.

v0:
```python
import jax
import jax.numpy as jnp
from jax import lax
from jax.sharding import PartitionSpec as P

HD = 128


def norm_reverse_pass(
    gradient_rows, normalized_gradient, unit_input_rows, reciprocal_deviation, norm_gain_vector
):
    scaled_gradient = normalized_gradient * norm_gain_vector
    inner_product = jnp.mean(scaled_gradient * unit_input_rows, axis=-1, keepdims=True)
    input_gradient = gradient_rows.astype(jnp.float32) + reciprocal_deviation * (
        scaled_gradient - unit_input_rows * inner_product
    )
    return (input_gradient, jnp.sum(normalized_gradient * unit_input_rows, axis=0))


def shards(
    inputs,
    norm_gain_vector,
    query_saved,
    key_saved,
    value_saved,
    w_query,
    w_key,
    w_value,
    w_out,
    output_gradient,
):
    single_float_type = jnp.float32
    brain_float_half = jnp.bfloat16
    length = inputs.shape[0]
    width = query_saved.shape[1]
    heads = width // HD
    widened_rows = inputs.astype(single_float_type)
    reciprocal_deviation = lax.rsqrt(
        jnp.mean(widened_rows * widened_rows, axis=-1, keepdims=True) + 1e-06
    )
    unit_input_rows = widened_rows * reciprocal_deviation
    normalized_rows = (unit_input_rows * norm_gain_vector).astype(brain_float_half)
    query = query_saved.reshape(length, heads, HD)
    keys = key_saved.reshape(length, heads, HD)
    values = value_saved.reshape(length, heads, HD)
    scores = jnp.einsum("qhd,khd->hqk", query, keys, preferred_element_type=single_float_type)
    probs = jax.nn.softmax(scores, axis=-1)
    probs_low = probs.astype(brain_float_half)
    attended = (
        jnp.einsum("hqk,khd->qhd", probs_low, values, preferred_element_type=single_float_type)
        .astype(brain_float_half)
        .reshape(length, width)
    )
    grad_att = jnp.einsum(
        "td,id->ti", output_gradient, w_out, preferred_element_type=single_float_type
    ).astype(brain_float_half)
    part_out = jnp.einsum(
        "ti,td->id", attended, output_gradient, preferred_element_type=single_float_type
    )
    grad_att3 = grad_att.reshape(length, heads, HD)
    grad_val = (
        jnp.einsum("hqk,qhd->khd", probs_low, grad_att3, preferred_element_type=single_float_type)
        .astype(brain_float_half)
        .reshape(length, width)
    )
    grad_prob = jnp.einsum(
        "qhd,khd->hqk", grad_att3, values, preferred_element_type=single_float_type
    )
    delta = jnp.sum(probs * grad_prob, axis=-1, keepdims=True)
    grad_score = (probs * (grad_prob - delta)).astype(brain_float_half)
    grad_query = (
        jnp.einsum("hqk,khd->qhd", grad_score, keys, preferred_element_type=single_float_type)
        .astype(brain_float_half)
        .reshape(length, width)
    )
    grad_key = (
        jnp.einsum("hqk,qhd->khd", grad_score, query, preferred_element_type=single_float_type)
        .astype(brain_float_half)
        .reshape(length, width)
    )
    part_query = jnp.einsum(
        "td,ti->di", normalized_rows, grad_query, preferred_element_type=single_float_type
    )
    part_key = jnp.einsum(
        "td,ti->di", normalized_rows, grad_key, preferred_element_type=single_float_type
    )
    part_value = jnp.einsum(
        "td,ti->di", normalized_rows, grad_val, preferred_element_type=single_float_type
    )
    total = jnp.einsum("ti,di->td", grad_query, w_query, preferred_element_type=single_float_type)
    total = total + jnp.einsum(
        "ti,di->td", grad_key, w_key, preferred_element_type=single_float_type
    )
    normalized_gradient = lax.psum(
        (
            total
            + jnp.einsum("ti,di->td", grad_val, w_value, preferred_element_type=single_float_type)
        ).astype(jnp.bfloat16),
        "mp",
    ).astype(jnp.float32)
    input_gradient, partial_gain = norm_reverse_pass(
        output_gradient,
        normalized_gradient,
        unit_input_rows,
        reciprocal_deviation,
        norm_gain_vector,
    )
    grad_inputs = input_gradient.astype(brain_float_half)
    sum_query, sum_key, sum_value, sum_out, sum_gain = (
        lax.psum(part_query.astype(jnp.bfloat16), "dp").astype(jnp.float32),
        lax.psum(part_key.astype(jnp.bfloat16), "dp").astype(jnp.float32),
        lax.psum(part_value.astype(jnp.bfloat16), "dp").astype(jnp.float32),
        lax.psum(part_out.astype(jnp.bfloat16), "dp").astype(jnp.float32),
        lax.psum(partial_gain.astype(jnp.bfloat16), "dp").astype(jnp.float32),
    )
    return (
        grad_inputs,
        sum_query.astype(brain_float_half),
        sum_key.astype(brain_float_half),
        sum_value.astype(brain_float_half),
        sum_out.astype(brain_float_half),
        sum_gain,
    )


def solution(mesh):
    return jax.shard_map(
        shards,
        mesh=mesh,
        in_specs=(
            P("dp", None),
            P(),
            P("dp", "mp"),
            P("dp", "mp"),
            P("dp", "mp"),
            P(None, "mp"),
            P(None, "mp"),
            P(None, "mp"),
            P("mp", None),
            P("dp", None),
        ),
        out_specs=(P("dp", None), P(None, "mp"), P(None, "mp"), P(None, "mp"), P("mp", None), P()),
        check_vma=False,
    )
```

profile of v0, /device:TPU:0, one launch (start us, length us, event | category | flops | bytes accessed | tf_op | source)
XLA Modules:
  0.0 488.0 jit_solution(1306815976802726831)
XLA Ops:
  7.2 0.0 all-reduce.4.cloned.1.call-start
  7.2 2.9 copy.32
  10.1 0.0 copy-start.7
  10.1 4.0 copy.33
  14.1 0.0 copy-done.7
  14.1 5.9 %convolution_convert_fusion.4 = bf16[512,2048]{1,0:T(8,128)(2,1)} fusion(bf16[512,1024]{1,0:T(8,128)(2,1)S(1)} %copy-done.7, bf16[2048,1024]{1,0:T(8,128)(2,1)} %param.18), kind=kOutput, calls=%fused_computation.13 | convolution fusion | flops 2148532224 | bytes 7340032 | tf_op jit(solution)/shard_map/td,id->ti/dot_general | solution.py:54
  20.0 3.9 copy.34
  23.9 3.9 copy.35
  27.8 9.4 %fusion.35 = (f32[16,512]{1,0:T(8,128)S(1)}, f32[16,512,512]{1,2,0:T(8,128)}) fusion(bf16[512,16,128]{0,2,1:T(8,128)(2,1)} %bitcast.47, bf16[512,16,128]{0,2,1:T(8,128)(2,1)S(1)} %bitcast.43), kind=kOutput, calls=%fused_computation.37 | convolution fusion | flops 1082130944 | bytes 21004288 | tf_op jit(solution)/shard_map/sub | solution.py:47
  37.2 12.3 %multiply_reduce_fusion = (f32[16,512]{1,0:T(8,128)S(1)}, f32[16,512,512]{1,2,0:T(8,128)}) fusion(f32[16,512,512]{1,2,0:T(8,128)} %get-tuple-element.13, f32[16,512]{1,0:T(8,128)S(1)} %get-tuple-element.12, bf16[512,16,128]{0,2,1:T(8,128)(2,1)} %bitcast.55, bf16[512,16,128]{0,2,1:T(8,128)(2,1)} %bitcast.53), kind=kOutput, calls=%fused_computation.2 | convolution fusion | flops 1086316544 | bytes 37814272 | tf_op jit(solution)/shard_map/qhd,khd->hqk/dot_general | solution.py:66
  49.5 11.6 %multiply_convert_fusion = bf16[16,512,512]{1,2,0:T(8,128)(2,1)S(1)} fusion(f32[16,512,512]{1,2,0:T(8,128)} %get-tuple-element.15, f32[16,512]{1,0:T(8,128)S(1)} %get-tuple-element.14, f32[16,512,512]{1,2,0:T(8,128)} %get-tuple-element.13, f32[16,512]{1,0:T(8,128)S(1)} %get-tuple-element.12), kind=kLoop, calls=%fused_computation.1 | loop fusion | flops 16777216 | bytes 42008576 | tf_op jit(solution)/shard_map/convert_element_type | solution.py:70
  61.1 5.7 %convolution_convert_fusion.6 = bf16[16,512,128]{1,2,0:T(8,128)(2,1)} fusion(bf16[16,512,512]{1,2,0:T(8,128)(2,1)S(1)} %multiply_convert_fusion, bf16[512,16,128]{0,2,1:T(8,128)(2,1)} %bitcast.48), kind=kOutput, calls=%fused_computation.33 | convolution fusion | flops 1074790400 | bytes 12582912 | tf_op jit(solution)/shard_map/hqk,qhd->khd/dot_general | solution.py:77
  66.8 2.6 convolution_convert_fusion.5
  69.4 10.4 %fusion.16 = bf16[16,128,512]{2,1,0:T(8,128)(2,1)} fusion(bf16[512,16,128]{0,2,1:T(8,128)(2,1)} %bitcast.56, f32[16,512]{1,0:T(8,128)S(1)} %get-tuple-element.12, bf16[512,16,128]{0,2,1:T(8,128)(2,1)} %bitcast.49, bf16[512,16,128]{0,2,1:T(8,128)(2,1)S(1)} %bitcast.45), kind=kOutput, calls=%fused_computation.30 | convolution fusion | flops 2161123840 | bytes 8421376 | tf_op jit(solution)/shard_map/hqk,qhd->khd/dot_general | solution.py:62
  79.7 0.0 copy-start.1
  79.7 0.0 copy-start.10
  79.7 5.3 %fusion.37 = f32[512,1024]{1,0:T(8,128)S(1)} fusion(bf16[512,2048]{0,1:T(8,128)(2,1)} %bitcast.59, bf16[1024,2048]{1,0:T(8,128)(2,1)} %param.16), kind=kOutput, calls=%fused_computation.39 | convolution fusion | flops 2147483648 | bytes 8388608 | tf_op jit(solution)/shard_map/ti,di->td/dot_general | solution.py:91
  85.1 0.0 copy-done.1
  85.1 0.0 copy-done.10
  85.1 0.0 copy-start.11
  85.1 0.0 copy-start.12
  85.1 2.4 fusion.36
  87.5 0.0 copy-done.11
  87.5 0.5 copy-done.12
  88.0 0.0 copy-start
  88.0 3.4 add_convert_fusion
  91.3 0.0 copy-start.9
  91.3 0.0 all-reduce.4.cloned.1.call-update
  91.4 10.9 %all-reduce.6.cloned.1.call-start = ((), (), s32[]{:S(2)}) async-start(), calls=%async_computation.1 | async-start | bytes 33554432 | tf_op jit(solution)/shard_map/psum | solution.py:110
  102.3 0.0 copy-done
  102.3 0.3 fusion.14
  102.6 0.0 copy-done.9
  102.6 0.0 copy-start.2
  102.6 6.4 %convolution_convert_fusion.2 = bf16[1024,2048]{1,0:T(8,128)(2,1)} fusion(bf16[512,2048]{0,1:T(8,128)(2,1)} %bitcast.60, bf16[512,1024]{1,0:T(8,128)(2,1)S(1)} %copy-done, f32[1024]{0:T(1024)S(1)} %copy-done.9, f32[512]{0:T(512)S(1)} %add_rsqrt_fusion), kind=kOutput, calls=%fused_computation.11 | convolution fusion | flops 2151677952 | bytes 7346176 | tf_op jit(solution)/shard_map/td,ti->di/dot_general | solution.py:84
  109.0 0.0 copy-done.2
  109.0 4.7 convolution_convert_fusion.3
  113.7 9.7 %fusion.19 = bf16[16,512,128]{1,2,0:T(8,128)(2,1)} fusion(bf16[512,16,128]{0,2,1:T(8,128)(2,1)} %bitcast.54, f32[16,512]{1,0:T(8,128)S(1)} %get-tuple-element.12, bf16[512,16,128]{0,2,1:T(8,128)(2,1)} %bitcast.50, bf16[512,16,128]{0,2,1:T(8,128)(2,1)S(1)} %bitcast.46), kind=kOutput, calls=%fused_computation.31 | convolution fusion | flops 2161123840 | bytes 8421376 | tf_op jit(solution)/shard_map/hqk,khd->qhd/dot_general | solution.py:50
  123.4 0.0 copy-start.13
  123.4 6.4 %convolution_convert_fusion = bf16[2048,1024]{1,0:T(8,128)(2,1)} fusion(bf16[512,2048]{0,1:T(8,128)(2,1)} %bitcast.61, bf16[512,1024]{1,0:T(8,128)(2,1)} %param.19), kind=kOutput, calls=%fused_computation.9 | convolution fusion | flops 2149580800 | bytes 7340032 | tf_op jit(solution)/shard_map/ti,td->id/dot_general | solution.py:57
  129.7 0.0 copy-done.13
  129.7 4.7 convolution_convert_fusion.1
  134.4 0.0 all-reduce.6.cloned.1.call-update
  134.4 0.0 copy-start.8
  134.4 18.7 %all-reduce.4.cloned.1.call-done = bf16[512,1024]{1,0:T(8,128)(2,1)} async-done(((bf16[512,1024]{1,0:T(8,128)(2,1)}), bf16[512,1024]{1,0:T(8,128)(2,1)}) %all-reduce.4.cloned.1.call-update) | async-done | bytes 1048592 | tf_op jit(solution)/shard_map/psum | solution.py:94
  153.1 0.0 copy-start.6
  153.1 2.1 fusion.15
  155.2 9.9 %psum.47 = bf16[1024]{0:T(1024)(128)(2,1)S(1)} all-reduce(bf16[1024]{0:T(1024)(128)(2,1)S(1)} %get-tuple-element.6), channel_id=1, replica_groups=mesh['dp'=4,'mp'=8] {'dp'}, use_global_device_ids=true, to_apply=%region_11.0 | all-reduce | flops 1024 | bytes 4096 | tf_op jit(solution)/shard_map/psum | solution.py:114
  165.1 0.6 convert_element_type.99
  165.7 0.0 copy-done.8
  165.7 0.0 copy-done.6
  165.7 1.7 fusion.11
  167.4 299.2 %all-reduce.6.cloned.1.call-done = (bf16[1024,2048]{1,0:T(8,128)(2,1)}, bf16[1024,2048]{1,0:T(8,128)(2,1)}, bf16[1024,2048]{1,0:T(8,128)(2,1)}, bf16[2048,1024]{1,0:T(8,128)(2,1)}) async-done(((bf16[1024,2048]{1,0:T(8,128)(2,1)}, bf16[1024,2048]{1,0:T(8,128)(2,1)}, bf16[1024,2048]{1,0:T(8,128)(2,1)}, bf16[2048,1024]{1,0:T(8,128)(2,1)}), (bf16[1024,2048]{1,0:T(8,128)(2,1)}, bf16[1024,2048]{1,0:T(8,128)(2,1)}, ...) | async-done | bytes 16777232 | tf_op jit(solution)/shard_map/psum | solution.py:110
  466.6 0.0 copy-start.5
  466.6 4.9 %copy.41 = bf16[1024,2048]{1,0:T(8,128)(2,1)} copy(bf16[1024,2048]{1,0:T(8,128)(2,1)} %get-tuple-element.17) | data formatting | bytes 8388608
  471.6 0.0 copy-done.5
  471.6 0.0 copy-start.4
  471.6 2.1 copy.42
  473.7 1.6 copy-done.4
  475.3 0.0 copy-start.3
  475.3 2.1 copy.43
  477.4 1.6 copy-done.3
  479.0 2.0 copy.44
  (2 shorter events, 0.0 us)
Async XLA Ops:
  7.2 145.9 %all-reduce.4.cloned.1.call-start = ((), (), s32[]{:S(2)}) async-start(), calls=%async_computation | async-start | bytes 2097152 | tf_op jit(solution)/shard_map/psum | solution.py:94
  10.1 4.0 copy-start.7
  79.7 5.4 %copy-start.1 = (bf16[16,512,128]{1,2,0:T(8,128)(2,1)S(1)}, bf16[16,512,128]{1,2,0:T(8,128)(2,1)}, u32[]{:S(2)}) copy-start(bf16[16,512,128]{1,2,0:T(8,128)(2,1)} %convolution_convert_fusion.5) | copy-start | bytes 6291460
  79.7 5.4 %copy-start.10 = (bf16[1024,2048]{1,0:T(8,128)(2,1)S(1)}, bf16[1024,2048]{1,0:T(8,128)(2,1)}, u32[]{:S(2)}) copy-start(bf16[1024,2048]{1,0:T(8,128)(2,1)} %param.15) | copy-start | bytes 12582916
  85.1 2.4 copy-start.11
  85.1 2.9 copy-start.12
  88.0 14.3 %copy-start = (bf16[512,1024]{1,0:T(8,128)(2,1)S(1)}, bf16[512,1024]{1,0:T(8,128)(2,1)}, u32[]{:S(2)}) copy-start(bf16[512,1024]{1,0:T(8,128)(2,1)} %param.10) | copy-start | bytes 3145732
  91.3 11.2 %copy-start.9 = (f32[1024]{0:T(1024)S(1)}, f32[1024]{0:T(1024)}, u32[]{:S(2)}) copy-start(f32[1024]{0:T(1024)} %param.11) | copy-start | bytes 12292
  91.4 375.3 %all-reduce.6.cloned.1.call-start = ((), (), s32[]{:S(2)}) async-start(), calls=%async_computation.1 | async-start | bytes 33554432 | tf_op jit(solution)/shard_map/psum | solution.py:110
  102.6 6.4 %copy-start.2 = (bf16[16,512,128]{1,2,0:T(8,128)(2,1)S(1)}, bf16[16,512,128]{1,2,0:T(8,128)(2,1)}, u32[]{:S(2)}) copy-start(bf16[16,512,128]{1,2,0:T(8,128)(2,1)} %convolution_convert_fusion.5) | copy-start | bytes 6291460
  123.4 6.4 %copy-start.13 = (bf16[16,128,512]{2,1,0:T(8,128)(2,1)S(1)}, bf16[16,128,512]{2,1,0:T(8,128)(2,1)}, u32[]{:S(2)}) copy-start(bf16[16,128,512]{2,1,0:T(8,128)(2,1)} %fusion.16) | copy-start | bytes 6291460
  134.4 31.3 %copy-start.8 = (bf16[512,1024]{1,0:T(8,128)(2,1)S(1)}, bf16[512,1024]{1,0:T(8,128)(2,1)}, u32[]{:S(2)}) copy-start(bf16[512,1024]{1,0:T(8,128)(2,1)} %param.19) | copy-start | bytes 3145732
  153.1 12.7 %copy-start.6 = (bf16[512,1024]{1,0:T(8,128)(2,1)S(1)}, bf16[512,1024]{1,0:T(8,128)(2,1)}, u32[]{:S(2)}) copy-start(bf16[512,1024]{1,0:T(8,128)(2,1)} %all-reduce.4.cloned.1.call-done) | copy-start | bytes 3145732
  466.6 4.9 %copy-start.5 = (bf16[1024,2048]{1,0:T(8,128)(2,1)S(1)}, bf16[1024,2048]{1,0:T(8,128)(2,1)}, u32[]{:S(2)}) copy-start(bf16[1024,2048]{1,0:T(8,128)(2,1)} %get-tuple-element.18) | copy-start | bytes 12582916
  471.6 3.7 copy-start.4
  475.3 3.7 copy-start.3
Sparse Core Ops, SparseCore 0:
  91.5 61.5 all-reduce.3
  157.7 308.9 all-reduce.5
where the time goes:
time: 496 us; the launch traced here: 488 us
  waiting for transfers between devices  318 us (64%)
  matrix products  89.1 us (18%)
  local copies, waits for them, and re-layouts  29.6 us (6%)
  other arithmetic  16.2 us (3%)
  between operations  14.4 us (3%)
  starting transfers between devices  10.9 us (2%)
  blocking collectives  9.92 us (2%)
    psum x1, waiting for transfers between devices, shards(): lax.psum(part_query.astype(jnp.bfloat16), 'dp').astype(jnp.float32)  299 us
    psum x1, waiting for transfers between devices, shards(): lax.psum((total + jnp.einsum('ti,di->td', grad_val, w_value, preferred_el...  18.7 us
    unnamed x32, local copies, waits for them, and re-layouts  14.9 us
    dot_general x1, matrix products, shards(): jnp.einsum('qhd,khd->hqk', grad_att3, values, preferred_element_type=sing...  12.3 us
    convert_element_type x1, other arithmetic, shards(): grad_score = (probs * (grad_prob - delta)).astype(brain_float_half)  11.6 us
    psum x1, starting transfers between devices, shards(): lax.psum(part_query.astype(jnp.bfloat16), 'dp').astype(jnp.float32)  10.9 us
    dot_general x1, matrix products, shards(): jnp.einsum('hqk,qhd->khd', probs_low, grad_att3, preferred_element_type=s...  10.4 us
    psum x1, blocking collectives, shards(): lax.psum(partial_gain.astype(jnp.bfloat16), 'dp').astype(jnp.float32)  9.92 us
  transfers between devices with their start and end apart: 2, of which 2 were waited for; matrix products, arithmetic and copies ran while one was open for 7% of the time, Pallas kernels for 0%

commit v1 on v0

--- a/solution.py
+++ b/solution.py
@@ -1,9 +1,15 @@
 import jax
 import jax.numpy as jnp
 from jax import lax
+from jax.experimental import pallas as pl
+from jax.experimental.pallas import tpu as pltpu
 from jax.sharding import PartitionSpec as P
 
 HD = 128
+N_DP = 4
+MESH = pl.DeviceIdType.MESH
+F32 = jnp.float32
+BF16 = jnp.bfloat16
 
 
 def norm_reverse_pass(
@@ -123,22 +129,412 @@
     )
 
 
+def dot_nn(a, b):
+    return lax.dot_general(a, b, (((1,), (0,)), ((), ())), preferred_element_type=F32)
+
+
+def dot_nt(a, b):
+    return lax.dot_general(a, b, (((1,), (1,)), ((), ())), preferred_element_type=F32)
+
+
+def dot_tn(a, b):
+    return lax.dot_general(a, b, (((0,), (0,)), ((), ())), preferred_element_type=F32)
+
+
+def flipped(me, mask):
+    x, y = me % 2, me // 2
+    bx, by = mask % 2, mask // 2
+    return (y + by * (1 - 2 * y)) * 2 + x + bx * (1 - 2 * x)
+
+
+def greet(partners):
+    barrier = pltpu.get_barrier_semaphore()
+    for partner in partners:
+        pl.semaphore_signal(barrier, inc=1, device_id=partner, device_id_type=MESH)
+    pl.semaphore_wait(barrier, len(partners))
+
+
+def attention_kernel(
+    q_ref, k_ref, v_ref, wq_ref, wk_ref, wv_ref, wo_ref, rows_ref,
+    grads_out, att_out, gathered_out, total_out,
+    grads_buf, att_buf, total,
+    a2a_send, a2a_recv, gather_send, gather_recv, local_sem,
+):
+    me, mp = lax.axis_index("dp"), lax.axis_index("mp")
+    core, half = mp % 2, (mp // 2) % 2
+    other_core = (me, mp + 1 - 2 * core)
+    other_z = (me, mp + 2 - 4 * half)
+    greet([(flipped(me, 1), mp), (flipped(me, 2), mp), (flipped(me, 3), mp), other_core, other_z])
+    depth = rows_ref.shape[1] // 2
+    steps = grads_buf.shape[0]
+
+    def gather_copy(slot, src, array, owner, part, target):
+        rows = pl.ds(pl.multiple_of(part * depth, depth), depth)
+        return pltpu.make_async_remote_copy(
+            src_ref=src.at[array, rows] if src is rows_ref else src.at[array, owner, rows],
+            dst_ref=gathered_out.at[array, owner, rows],
+            send_sem=gather_send.at[slot],
+            recv_sem=gather_recv.at[slot],
+            device_id=target,
+            device_id_type=MESH,
+        )
+
+    def spread(mask):
+        return gather_copy(mask - 1, rows_ref, core, me, half, (flipped(me, mask), mp))
+
+    def along_z(mask):
+        return gather_copy(2 + mask, gathered_out, core, flipped(me, mask), half, other_z)
+
+    def across(mask, second):
+        part = 1 - half if second else half
+        return gather_copy(
+            5 + mask + 3 * second, gathered_out, core, flipped(me, mask), part, other_core
+        )
+
+    def own_rows(array):
+        return pltpu.make_async_copy(
+            rows_ref.at[array], gathered_out.at[array, me], local_sem.at[array]
+        )
+
+    for mask in (1, 2, 3):
+        spread(mask).start()
+    own_rows(0).start()
+    own_rows(1).start()
+
+    def place(step):
+        return step // N_DP, flipped(me, (step % N_DP + 1) % N_DP)
+
+    def remote(step):
+        k, target = place(step)
+        return [
+            pltpu.make_async_remote_copy(
+                src_ref=buf.at[step],
+                dst_ref=out.at[k, me],
+                send_sem=a2a_send.at[i, step],
+                recv_sem=a2a_recv.at[i, step],
+                device_id=(target, mp),
+                device_id_type=MESH,
+            )
+            for i, (buf, out) in enumerate(((grads_buf, grads_out), (att_buf, att_out)))
+        ]
+
+    def local(step):
+        k, _ = place(step)
+        return [
+            pltpu.make_async_copy(buf.at[step], out.at[k, me], a2a_send.at[i, step])
+            for i, (buf, out) in enumerate(((grads_buf, grads_out), (att_buf, att_out)))
+        ]
+
+    total[...] = jnp.zeros_like(total)
+    per_chunk = steps // N_DP
+
+    def head_step(step, carry):
+        k, target = place(step)
+        cols = pl.ds(pl.multiple_of((target * per_chunk + k) * HD, HD), HD)
+        query, keys, values = q_ref[:, cols], k_ref[:, cols], v_ref[:, cols]
+        grad_att = dot_nn(wo_ref[cols, :], rows_ref[1]).astype(BF16)
+        scores = dot_nt(keys, query)
+        weights = jnp.exp(scores - jnp.max(scores, axis=0, keepdims=True))
+        probs = weights * (1.0 / jnp.sum(weights, axis=0, keepdims=True))
+        probs_low = probs.astype(BF16)
+        att_buf[step] = dot_tn(values, probs_low).astype(BF16)
+        grad_val = dot_nt(probs_low, grad_att).astype(BF16)
+        grad_prob = dot_nn(values, grad_att)
+        delta = jnp.sum(probs * grad_prob, axis=0, keepdims=True)
+        grad_score = (probs * (grad_prob - delta)).astype(BF16)
+        grad_query = jnp.transpose(dot_tn(keys, grad_score)).astype(BF16)
+        grad_key = dot_nn(grad_score, query).astype(BF16)
+        grads = jnp.concatenate([grad_query, grad_key, grad_val], axis=1)
+        grads_buf[step] = grads
+
+        @pl.when(step % N_DP != N_DP - 1)
+        def _():
+            for copy in remote(step):
+                copy.start()
+
+        @pl.when(step % N_DP == N_DP - 1)
+        def _():
+            for copy in local(step):
+                copy.start()
+
+        projections = jnp.concatenate([wq_ref[:, cols], wk_ref[:, cols], wv_ref[:, cols]], axis=1)
+        total[...] += dot_nt(grads, projections)
+        return carry
+
+    lax.fori_loop(0, steps // 2, head_step, 0)
+    for mask in (1, 2, 3):
+        spread(mask).wait_recv()
+        along_z(mask).start()
+        across(mask, 0).start()
+    lax.fori_loop(steps // 2, steps, head_step, 0)
+    total_out[...] = total[...].astype(BF16)
+    for mask in (1, 2, 3):
+        along_z(mask).wait_recv()
+        across(mask, 1).start()
+
+    def drain(step, carry):
+        @pl.when(step % N_DP != N_DP - 1)
+        def _():
+            for copy in remote(step):
+                copy.wait()
+
+        @pl.when(step % N_DP == N_DP - 1)
+        def _():
+            for copy in local(step):
+                copy.wait()
+
+        return carry
+
+    lax.fori_loop(0, steps, drain, 0)
+    for mask in (1, 2, 3):
+        spread(mask).wait_send()
+        along_z(mask).wait_send()
+        across(mask, 0).wait()
+        across(mask, 1).wait()
+    own_rows(0).wait()
+    own_rows(1).wait()
+
+
+def weight_kernel(
+    grads_ref, att_ref, gathered_ref,
+    gq_out, gk_out, gv_out, go_out,
+    wide, tall,
+    send_sem, recv_sem, local_sem,
+):
+    me, mp = lax.axis_index("dp"), lax.axis_index("mp")
+    peer_x, peer_y = flipped(me, 1), flipped(me, 2)
+    greet([(peer_x, mp), (peer_y, mp)])
+    per_chunk = grads_ref.shape[0]
+    pieces = wide.shape[1]
+    height, width = wide.shape[2], wide.shape[3]
+    outs = (gq_out, gk_out, gv_out, go_out)
+
+    def spot(array, piece, owner, part=None):
+        if array < 3:
+            first, size = piece * height, height
+            cols = pl.ds(pl.multiple_of(owner * width, width), width)
+        else:
+            first, size = (owner * per_chunk + piece) * HD, HD
+            cols = slice(None)
+        if part is not None:
+            size = size // 2
+            first = first + part * size
+        return outs[array].at[pl.ds(pl.multiple_of(first, size), size), cols]
+
+    def staged(array, piece):
+        return wide.at[array, piece] if array < 3 else tall.at[piece]
+
+    def copy_to(kind, array, piece, src, dst, peer):
+        return pltpu.make_async_remote_copy(
+            src_ref=src,
+            dst_ref=dst,
+            send_sem=send_sem.at[kind, array, piece],
+            recv_sem=recv_sem.at[kind, array, piece],
+            device_id=(peer, mp),
+            device_id_type=MESH,
+        )
+
+    def own(kind, array, piece):
+        return copy_to(
+            kind, array, piece, staged(array, piece), spot(array, piece, me), (peer_x, peer_y)[kind]
+        )
+
+    def forward(kind, array, piece):
+        block = spot(array, piece, (peer_x, peer_y)[kind], kind)
+        return copy_to(2 + kind, array, piece, block, block, (peer_y, peer_x)[kind])
+
+    def keep(array, piece):
+        return pltpu.make_async_copy(
+            staged(array, piece), spot(array, piece, me), local_sem.at[array, piece]
+        )
+
+    def send(array, piece):
+        own(0, array, piece).start()
+        own(1, array, piece).start()
+        keep(array, piece).start()
+
+    for array in range(3):
+        lanes = slice(array * HD, (array + 1) * HD)
+
+        def wide_step(piece, carry, array=array, lanes=lanes):
+            rows = pl.ds(pl.multiple_of(piece * height, height), height)
+            acc = None
+            for owner in range(N_DP):
+                right = jnp.concatenate(
+                    [grads_ref[k, owner, :, lanes] for k in range(per_chunk)], axis=1
+                )
+                term = dot_nn(gathered_ref[0, owner, rows, :], right)
+                acc = term if acc is None else acc + term
+            wide[array, piece] = acc.astype(BF16)
+            send(array, piece)
+            return carry
+
+        lax.fori_loop(0, pieces, wide_step, 0)
+
+    def tall_step(piece, carry):
+        acc = None
+        for owner in range(N_DP):
+            term = dot_nt(att_ref[piece, owner], gathered_ref[1, owner])
+            acc = term if acc is None else acc + term
+        tall[piece] = acc.astype(BF16)
+        send(3, piece)
+        return carry
+
+    lax.fori_loop(0, per_chunk, tall_step, 0)
+
+    def count(array):
+        return pieces if array < 3 else per_chunk
+
+    for array in range(4):
+
+        def pass_on(piece, carry, array=array):
+            for kind in (0, 1):
+                own(kind, array, piece).wait_recv()
+                forward(kind, array, piece).start()
+            return carry
+
+        lax.fori_loop(0, count(array), pass_on, 0)
+    for array in range(4):
+
+        def finish(piece, carry, array=array):
+            for kind in (0, 1):
+                own(kind, array, piece).wait_send()
+                forward(kind, array, piece).wait()
+            keep(array, piece).wait()
+            return carry
+
+        lax.fori_loop(0, count(array), finish, 0)
+
+
+def fused_grads(
+    normalized_rows, query_saved, key_saved, value_saved, w_query, w_key, w_value, w_out, output_gradient
+):
+    length, width = query_saved.shape
+    features = normalized_rows.shape[1]
+    steps = width // HD
+    per_chunk = steps // N_DP
+    rows = jnp.stack([normalized_rows.T, output_gradient.T])
+    vmem, hbm = pl.BlockSpec(memory_space=pltpu.VMEM), pl.BlockSpec(memory_space=pl.ANY)
+    dma = pltpu.SemaphoreType.DMA
+    grads, att, gathered, total = pl.pallas_call(
+        attention_kernel,
+        out_shape=(
+            jax.ShapeDtypeStruct((per_chunk, N_DP, length, 3 * HD), BF16),
+            jax.ShapeDtypeStruct((per_chunk, N_DP, HD, length), BF16),
+            jax.ShapeDtypeStruct((2, N_DP, features, length), BF16),
+            jax.ShapeDtypeStruct((length, features), BF16),
+        ),
+        in_specs=[vmem] * 8,
+        out_specs=(hbm, hbm, hbm, vmem),
+        scratch_shapes=[
+            pltpu.VMEM((steps, length, 3 * HD), BF16),
+            pltpu.VMEM((steps, HD, length), BF16),
+            pltpu.VMEM((length, features), F32),
+            dma((2, steps)),
+            dma((2, steps)),
+            dma((12,)),
+            dma((12,)),
+            dma((2,)),
+        ],
+        compiler_params=pltpu.CompilerParams(
+            collective_id=0, has_side_effects=True, vmem_limit_bytes=56 * 2**20
+        ),
+        cost_estimate=pl.CostEstimate(
+            flops=30 * length * width * features, bytes_accessed=40 * 2**20, transcendentals=0
+        ),
+    )(query_saved, key_saved, value_saved, w_query, w_key, w_value, w_out, rows)
+    pieces = 4
+    outs = pl.pallas_call(
+        weight_kernel,
+        out_shape=(jax.ShapeDtypeStruct((features, width), BF16),) * 3
+        + (jax.ShapeDtypeStruct((width, features), BF16),),
+        in_specs=[vmem] * 3,
+        out_specs=(hbm,) * 4,
+        scratch_shapes=[
+            pltpu.VMEM((3, pieces, features // pieces, per_chunk * HD), BF16),
+            pltpu.VMEM((per_chunk, HD, features), BF16),
+            dma((4, 4, max(pieces, per_chunk))),
+            dma((4, 4, max(pieces, per_chunk))),
+            dma((4, max(pieces, per_chunk))),
+        ],
+        compiler_params=pltpu.CompilerParams(
+            collective_id=1, has_side_effects=True, vmem_limit_bytes=48 * 2**20
+        ),
+        cost_estimate=pl.CostEstimate(
+            flops=200 * length * width * features, bytes_accessed=200 * 2**20, transcendentals=0
+        ),
+    )(grads, att, gathered)
+    return total, outs
+
+
+def fused_shards(
+    inputs,
+    norm_gain_vector,
+    query_saved,
+    key_saved,
+    value_saved,
+    w_query,
+    w_key,
+    w_value,
+    w_out,
+    output_gradient,
+):
+    widened_rows = inputs.astype(F32)
+    reciprocal_deviation = lax.rsqrt(
+        jnp.mean(widened_rows * widened_rows, axis=-1, keepdims=True) + 1e-06
+    )
+    unit_input_rows = widened_rows * reciprocal_deviation
+    normalized_rows = (unit_input_rows * norm_gain_vector).astype(BF16)
+    total, outs = fused_grads(
+        normalized_rows, query_saved, key_saved, value_saved, w_query, w_key, w_value, w_out,
+        output_gradient,
+    )
+    normalized_gradient = lax.psum(total, "mp").astype(F32)
+    input_gradient, partial_gain = norm_reverse_pass(
+        output_gradient,
+        normalized_gradient,
+        unit_input_rows,
+        reciprocal_deviation,
+        norm_gain_vector,
+    )
+    sum_gain = lax.psum(partial_gain.astype(BF16), "dp").astype(F32)
+    return (input_gradient.astype(BF16), *outs, sum_gain)
+
+
+def fits(mesh, arguments):
+    length, width = arguments[2].shape
+    n_dp, n_mp = mesh.shape["dp"], mesh.shape["mp"]
+    return (
+        n_dp == N_DP
+        and n_mp % 4 == 0
+        and width % (n_mp * N_DP * HD) == 0
+        and width <= 2048 * n_mp
+        and length == 512 * n_dp
+        and arguments[0].shape[1] == 1024
+    )
+
+
 def solution(mesh):
-    return jax.shard_map(
-        shards,
-        mesh=mesh,
-        in_specs=(
-            P("dp", None),
-            P(),
-            P("dp", "mp"),
-            P("dp", "mp"),
-            P("dp", "mp"),
-            P(None, "mp"),
-            P(None, "mp"),
-            P(None, "mp"),
-            P("mp", None),
-            P("dp", None),
-        ),
-        out_specs=(P("dp", None), P(None, "mp"), P(None, "mp"), P(None, "mp"), P("mp", None), P()),
-        check_vma=False,
-    )
+    def whole(*arguments):
+        return jax.shard_map(
+            fused_shards if fits(mesh, arguments) else shards,
+            mesh=mesh,
+            in_specs=(
+                P("dp", None),
+                P(),
+                P("dp", "mp"),
+                P("dp", "mp"),
+                P("dp", "mp"),
+                P(None, "mp"),
+                P(None, "mp"),
+                P(None, "mp"),
+                P("mp", None),
+                P("dp", None),
+            ),
+            out_specs=(
+                P("dp", None), P(None, "mp"), P(None, "mp"), P(None, "mp"), P("mp", None), P(),
+            ),
+            check_vma=False,
+        )(*arguments)
+
+    return whole

time: 496 us -> 324 us (0.65); the launches traced: 488 us -> 323 us
  waiting for transfers between devices: 318 us -> 0.04 us
  Pallas kernels: 0 us -> 272 us
  matrix products: 89.1 us -> 0 us
  starting transfers between devices: 10.9 us -> 0.04 us
  other arithmetic: 16.2 us -> 6.58 us
  local copies, waits for them, and re-layouts: 29.6 us -> 21.2 us
    psum x2 -> x1, waiting for transfers between devices: 318 us -> 0.02 us  [fused_shards(): normalized_gradient = lax.psum(total, 'mp').astype(F32)]
    pallas_call x0 -> x2, Pallas kernels: none -> 272 us  [the longest x1 144 us: fused_grads(): pl.pallas_call(weight_kernel, out_shape=(jax.ShapeDtypeStruct((features,...]
    dot_general x13 -> x0, matrix products: 79.7 us -> none  [the longest x1 12.3 us: shards(): jnp.einsum('qhd,khd->hqk', grad_att3, values, preferred_element_type=sing...]
    reshape x4 -> x0, local copies, waits for them, and re-layouts: 14.7 us -> none  [the longest x1 4.01 us: shards(): query = query_saved.reshape(length, heads, HD)]
    convert_element_type x3 -> x2, other arithmetic: 13.8 us -> 2.25 us  [the longest x1 1.65 us: fused_shards(): return (input_gradient.astype(BF16), *outs, sum_gain)]
    psum x2 -> x1, starting transfers between devices: 10.9 us -> 0.04 us  [fused_shards(): normalized_gradient = lax.psum(total, 'mp').astype(F32)]
    sub x1 -> x0, matrix products: 9.39 us -> none  [shards(): probs = jax.nn.softmax(scores, axis=-1)]
    unnamed x32 -> x35, local copies, waits for them, and re-layouts: 14.9 us -> 18.8 us
  transfers between devices with their start and end apart: 2 -> 1, of which waited for: 2 -> 0; matrix products, arithmetic and copies ran while one was open for 7% -> 0% of each run, Pallas kernels for 0% -> 44%
where the time goes in v1:
time: 324 us; the launch traced here: 323 us
  Pallas kernels  272 us (84%)
  local copies, waits for them, and re-layouts  21.2 us (7%)
  between operations  14.2 us (4%)
  blocking collectives  8.9 us (3%)
  other arithmetic  6.58 us (2%)
    pallas_call x1, Pallas kernels, fused_grads(): pl.pallas_call(weight_kernel, out_shape=(jax.ShapeDtypeStruct((features,...  144 us
    pallas_call x1, Pallas kernels, fused_grads(): pl.pallas_call(attention_kernel, out_shape=(jax.ShapeDtypeStruct((per_chu...  129 us
    unnamed x35, local copies, waits for them, and re-layouts  18.8 us
    psum x1, blocking collectives, fused_shards(): sum_gain = lax.psum(partial_gain.astype(BF16), 'dp').astype(F32)  8.9 us
  transfers between devices with their start and end apart: 1, of which 0 were waited for; matrix products, arithmetic and copies ran while one was open for 0% of the time, Pallas kernels for 44%

profile of v1, /device:TPU:0, one launch (start us, length us, event | category | flops | bytes accessed | tf_op | source)
XLA Modules:
  0.0 323.4 jit_solution(18172814545312320584)
XLA Ops:
  7.2 0.0 copy-start.9
  7.2 0.0 all-reduce.2.cloned.1.call-start
  7.2 1.6 copy.17
  8.8 0.0 copy-start.1
  8.8 0.0 copy-start.10
  8.8 0.3 fusion.9
  9.1 0.0 copy-done.9
  9.1 0.0 copy-start.12
  9.1 0.5 copy.16
  9.7 0.0 copy-done.10
  9.7 0.0 copy-start.3
  9.7 0.3 fusion.11
  10.0 0.0 copy-done.1
  10.0 0.0 copy-done.12
  10.0 1.5 pad_maximum_fusion.rows_ref
  11.5 0.0 copy-done.3
  11.5 128.5 %shard_map.145 = (bf16[4,4,512,384]{3,2,1,0:T(8,128)(2,1)}, bf16[4,4,128,512]{3,2,1,0:T(8,128)(2,1)}, bf16[2,4,1024,512]{3,2,1,0:T(8,128)(2,1)}, bf16[512,1024]{1,0:T(8,128)(2,1)}) custom-call(bf16[512,2048]{1,0:T(8,128)(2,1)} %q_ref.1, bf16[512,2048]{1,0:T(8,128)(2,1)} %k_ref.1, bf16[512,2048]{1,0:T(8,128)(2,1)} %v_ref.1, bf16[1024,2048]{1,0:T(8,128)(2,1)} %wq_ref.1, ...), custom_call_target="tpu_custom_call" | custom-call | flops 32212254720 | bytes 41943040 | tf_op jit(solution)/shard_map/pallas_call | solution.py:419
  140.1 0.0 copy-start
  140.1 2.4 copy.19
  142.5 0.0 all-reduce.2.cloned.1.call-update
  142.5 0.0 copy-done
  142.5 0.0 copy-start.2
  142.6 0.0 copy-start.11
  142.6 0.0 copy-start.13
  142.6 143.8 %shard_map.146 = (bf16[1024,2048]{1,0:T(8,128)(2,1)}, bf16[1024,2048]{1,0:T(8,128)(2,1)}, bf16[1024,2048]{1,0:T(8,128)(2,1)}, bf16[2048,1024]{1,0:T(8,128)(2,1)}) custom-call(bf16[4,4,512,384]{3,2,1,0:T(8,128)(2,1)} %get-tuple-element.15.grads_ref, bf16[4,4,128,512]{3,2,1,0:T(8,128)(2,1)S(1)} %copy-done, bf16[2,4,1024,512]{3,2,1,0:T(8,128)(2,1)} %get-tuple-element.17.gathered_ref), custom_call_target="tpu_custom_call" | custom-call | flops 214748364800 | bytes 209715200 | tf_op jit(solution)/shard_map/pallas_call | solution.py:447
  286.4 0.0 copy-start.4
  286.4 0.0 all-reduce.2.cloned.1.call-done
  286.4 0.0 copy-done.2
  286.4 0.0 copy-done.11
  286.4 0.0 copy-done.13
  286.5 0.0 copy-start.8
  286.5 2.2 fusion.10
  288.7 0.0 copy-done.4
  288.7 0.0 copy-done.8
  288.7 1.7 fusion.6
  290.4 2.3 copy.20
  292.7 8.9 %psum.15 = bf16[1024]{0:T(1024)(128)(2,1)S(1)} all-reduce(bf16[1024]{0:T(1024)(128)(2,1)S(1)} %get-tuple-element.28), channel_id=1, replica_groups=mesh['dp'=4,'mp'=8] {'dp'}, use_global_device_ids=true, to_apply=%region_4.0 | all-reduce | flops 1024 | bytes 4096 | tf_op jit(solution)/shard_map/psum | solution.py:500
  301.6 0.6 convert_element_type.27
  302.2 0.0 copy-start.7
  302.2 4.9 %copy.26 = bf16[1024,2048]{1,0:T(8,128)(2,1)} copy(bf16[1024,2048]{1,0:T(8,128)(2,1)} %get-tuple-element.37) | data formatting | bytes 8388608
  307.1 0.0 copy-done.7
  307.1 0.0 copy-start.6
  307.1 2.1 copy.27
  309.2 1.6 copy-done.6
  310.8 0.0 copy-start.5
  310.8 2.1 copy.28
  312.9 1.6 copy-done.5
  314.5 2.0 copy.29
  (2 shorter events, 0.0 us)
Async XLA Ops:
  7.2 2.0 copy-start.9
  7.2 279.2 %all-reduce.2.cloned.1.call-start = ((), (), s32[]{:S(2)}) async-start(), calls=%async_computation | async-start | bytes 2097152 | tf_op jit(solution)/shard_map/psum | solution.py:492
  8.8 1.2 copy-start.1
  8.8 0.9 copy-start.10
  9.1 0.9 copy-start.12
  9.7 1.8 copy-start.3
  140.1 2.5 copy-start
  142.5 143.9 %copy-start.2 = (bf16[512,1024]{0,1:T(8,128)(2,1)S(1)}, bf16[512,1024]{0,1:T(8,128)(2,1)}, u32[]{:S(2)}) copy-start(bf16[512,1024]{0,1:T(8,128)(2,1)} %copy-done.1) | copy-start | bytes 3145732
  142.6 143.9 %copy-start.11 = (f32[1024]{0:T(1024)S(1)}, f32[1024]{0:T(1024)}, u32[]{:S(2)}) copy-start(f32[1024]{0:T(1024)} %param.11) | copy-start | bytes 12292
  142.6 143.9 %copy-start.13 = (f32[512]{0:T(512)S(1)}, f32[512]{0:T(512)}, u32[]{:S(2)}) copy-start(f32[512]{0:T(512)} %copy-done.12) | copy-start | bytes 6148
  286.4 2.3 copy-start.4
  286.5 2.3 copy-start.8
  302.2 4.9 %copy-start.7 = (bf16[1024,2048]{1,0:T(8,128)(2,1)S(1)}, bf16[1024,2048]{1,0:T(8,128)(2,1)}, u32[]{:S(2)}) copy-start(bf16[1024,2048]{1,0:T(8,128)(2,1)} %get-tuple-element.38) | copy-start | bytes 12582916
  307.1 3.7 %copy-start.6 = (bf16[1024,2048]{1,0:T(8,128)(2,1)S(1)}, bf16[1024,2048]{1,0:T(8,128)(2,1)}, u32[]{:S(2)}) copy-start(bf16[1024,2048]{1,0:T(8,128)(2,1)} %get-tuple-element.39) | copy-start | bytes 12582916
  310.8 3.7 %copy-start.5 = (bf16[2048,1024]{1,0:T(8,128)(2,1)S(1)}, bf16[2048,1024]{1,0:T(8,128)(2,1)}, u32[]{:S(2)}) copy-start(bf16[2048,1024]{1,0:T(8,128)(2,1)} %get-tuple-element.40) | copy-start | bytes 12582916
Sparse Core Ops, SparseCore 0:
  142.7 59.0 all-reduce.1

commit v2 on v1

--- a/solution.py
+++ b/solution.py
@@ -1,3 +1,5 @@
+import functools
+
 import jax
 import jax.numpy as jnp
 from jax import lax
@@ -155,17 +157,38 @@
 
 
 def attention_kernel(
-    q_ref, k_ref, v_ref, wq_ref, wk_ref, wv_ref, wo_ref, rows_ref,
+    n_mp,
+    q_hbm, k_hbm, v_hbm, wq_hbm, wk_hbm, wv_hbm, wo_hbm, rows_ref,
     grads_out, att_out, gathered_out, total_out,
+    q_ref, k_ref, v_ref, wq_ref, wk_ref, wv_ref, wo_ref,
     grads_buf, att_buf, total,
-    a2a_send, a2a_recv, gather_send, gather_recv, local_sem,
+    a2a_send, a2a_recv, gather_send, gather_recv, local_sem, load_sem,
 ):
     me, mp = lax.axis_index("dp"), lax.axis_index("mp")
-    core, half = mp % 2, (mp // 2) % 2
+    parts = n_mp // 2
+    core, z = mp % 2, mp // 2
     other_core = (me, mp + 1 - 2 * core)
-    other_z = (me, mp + 2 - 4 * half)
-    greet([(flipped(me, 1), mp), (flipped(me, 2), mp), (flipped(me, 3), mp), other_core, other_z])
-    depth = rows_ref.shape[1] // 2
+    loads = [
+        pltpu.make_async_copy(src, dst, load_sem.at[i])
+        for i, (src, dst) in enumerate(
+            (
+                (q_hbm, q_ref), (k_hbm, k_ref), (v_hbm, v_ref), (wo_hbm, wo_ref),
+                (wq_hbm, wq_ref), (wk_hbm, wk_ref), (wv_hbm, wv_ref),
+            )
+        )
+    ]
+    for load in loads:
+        load.start()
+
+    def along(j):
+        return (me, (z + j) % parts * 2 + core)
+
+    greet(
+        [(flipped(me, mask), mp) for mask in (1, 2, 3)]
+        + [other_core]
+        + [along(j) for j in range(1, parts)]
+    )
+    depth = rows_ref.shape[1] // parts
     steps = grads_buf.shape[0]
 
     def gather_copy(slot, src, array, owner, part, target):
@@ -180,15 +203,17 @@
         )
 
     def spread(mask):
-        return gather_copy(mask - 1, rows_ref, core, me, half, (flipped(me, mask), mp))
-
-    def along_z(mask):
-        return gather_copy(2 + mask, gathered_out, core, flipped(me, mask), half, other_z)
-
-    def across(mask, second):
-        part = 1 - half if second else half
+        return gather_copy(mask - 1, rows_ref, core, me, z, (flipped(me, mask), mp))
+
+    def along_z(mask, j):
         return gather_copy(
-            5 + mask + 3 * second, gathered_out, core, flipped(me, mask), part, other_core
+            3 * j + mask - 1, gathered_out, core, flipped(me, mask), z, along(j)
+        )
+
+    def across(mask, j):
+        return gather_copy(
+            3 * (parts + j) + mask - 1, gathered_out, core, flipped(me, mask),
+            (z - j + parts) % parts, other_core,
         )
 
     def own_rows(array):
@@ -226,6 +251,8 @@
         ]
 
     total[...] = jnp.zeros_like(total)
+    for load in loads[:4]:
+        load.wait()
     per_chunk = steps // N_DP
 
     def head_step(step, carry):
@@ -257,20 +284,27 @@
             for copy in local(step):
                 copy.start()
 
+        @pl.when(step == 0)
+        def _():
+            for load in loads[4:]:
+                load.wait()
+
         projections = jnp.concatenate([wq_ref[:, cols], wk_ref[:, cols], wv_ref[:, cols]], axis=1)
         total[...] += dot_nt(grads, projections)
         return carry
 
-    lax.fori_loop(0, steps // 2, head_step, 0)
+    lax.fori_loop(0, N_DP, head_step, 0)
     for mask in (1, 2, 3):
         spread(mask).wait_recv()
-        along_z(mask).start()
+        for j in range(1, parts):
+            along_z(mask, j).start()
         across(mask, 0).start()
-    lax.fori_loop(steps // 2, steps, head_step, 0)
+    lax.fori_loop(N_DP, steps, head_step, 0)
     total_out[...] = total[...].astype(BF16)
-    for mask in (1, 2, 3):
-        along_z(mask).wait_recv()
-        across(mask, 1).start()
+    for j in range(1, parts):
+        for mask in (1, 2, 3):
+            along_z(mask, j).wait_recv()
+            across(mask, j).start()
 
     def drain(step, carry):
         @pl.when(step % N_DP != N_DP - 1)
@@ -288,22 +322,87 @@
     lax.fori_loop(0, steps, drain, 0)
     for mask in (1, 2, 3):
         spread(mask).wait_send()
-        along_z(mask).wait_send()
-        across(mask, 0).wait()
-        across(mask, 1).wait()
+        for j in range(1, parts):
+            along_z(mask, j).wait_send()
+        for j in range(parts):
+            across(mask, j).wait()
     own_rows(0).wait()
     own_rows(1).wait()
 
 
 def weight_kernel(
-    grads_ref, att_ref, gathered_ref,
-    gq_out, gk_out, gv_out, go_out,
-    wide, tall,
-    send_sem, recv_sem, local_sem,
+    n_mp,
+    grads_ref, att_hbm, gathered_hbm, total_ref, inputs_ref, outgrad_ref, gain_ref,
+    gq_out, gk_out, gv_out, go_out, gi_out, gain_out,
+    att_ref, gathered_ref, wide, tall, landing, gi_buf, gain_slots, gain_seqs,
+    send_sem, recv_sem, local_sem, load_sem,
+    total_send, total_recv, gi_send, gi_recv, slot_send, slot_recv, seq_send, seq_recv,
 ):
     me, mp = lax.axis_index("dp"), lax.axis_index("mp")
     peer_x, peer_y = flipped(me, 1), flipped(me, 2)
-    greet([(peer_x, mp), (peer_y, mp)])
+    loads = [
+        pltpu.make_async_copy(gathered_hbm.at[0], gathered_ref.at[0], load_sem.at[0]),
+        pltpu.make_async_copy(att_hbm, att_ref, load_sem.at[1]),
+        pltpu.make_async_copy(gathered_hbm.at[1], gathered_ref.at[1], load_sem.at[2]),
+    ]
+    for load in loads:
+        load.start()
+
+    def ahead(i):
+        return (mp + i) % n_mp
+
+    greet(
+        [(flipped(me, mask), mp) for mask in (1, 2, 3)] + [(me, ahead(i)) for i in range(1, n_mp)]
+    )
+    share = total_ref.shape[0] // n_mp
+
+    def rows_of(index):
+        return pl.ds(pl.multiple_of(index * share, share), share)
+
+    def total_copy(i):
+        return pltpu.make_async_remote_copy(
+            src_ref=total_ref.at[rows_of(ahead(i))],
+            dst_ref=landing.at[i],
+            send_sem=total_send.at[i],
+            recv_sem=total_recv.at[i],
+            device_id=(me, ahead(i)),
+            device_id_type=MESH,
+        )
+
+    def gi_copy(i):
+        return pltpu.make_async_remote_copy(
+            src_ref=gi_buf,
+            dst_ref=gi_out.at[rows_of(mp)],
+            send_sem=gi_send.at[i],
+            recv_sem=gi_recv.at[i],
+            device_id=(me, ahead(i)),
+            device_id_type=MESH,
+        )
+
+    def slot_copy(i):
+        return pltpu.make_async_remote_copy(
+            src_ref=gain_slots.at[mp],
+            dst_ref=gain_slots.at[mp],
+            send_sem=slot_send.at[i],
+            recv_sem=slot_recv.at[i],
+            device_id=(me, ahead(i)),
+            device_id_type=MESH,
+        )
+
+    def seq_copy(mask):
+        return pltpu.make_async_remote_copy(
+            src_ref=gain_seqs.at[me],
+            dst_ref=gain_seqs.at[me],
+            send_sem=seq_send.at[mask],
+            recv_sem=seq_recv.at[mask],
+            device_id=(flipped(me, mask), mp),
+            device_id_type=MESH,
+        )
+
+    gi_keep = pltpu.make_async_copy(gi_buf, gi_out.at[rows_of(mp)], gi_send.at[0])
+    others = range(1, n_mp)
+    for i in others:
+        total_copy(i).start()
     per_chunk = grads_ref.shape[0]
     pieces = wide.shape[1]
     height, width = wide.shape[2], wide.shape[3]
@@ -353,6 +452,7 @@
         own(1, array, piece).start()
         keep(array, piece).start()
 
+    loads[0].wait()
     for array in range(3):
         lanes = slice(array * HD, (array + 1) * HD)
 
@@ -371,6 +471,9 @@
 
         lax.fori_loop(0, pieces, wide_step, 0)
 
+    loads[1].wait()
+    loads[2].wait()
+
     def tall_step(piece, carry):
         acc = None
         for owner in range(N_DP):
@@ -382,6 +485,22 @@
 
     lax.fori_loop(0, per_chunk, tall_step, 0)
 
+    normed_grad = total_ref[rows_of(mp), :].astype(F32)
+    for i in others:
+        total_copy(i).wait_recv()
+        normed_grad += landing[i].astype(F32)
+    saved = inputs_ref[rows_of(mp), :].astype(F32)
+    rstd = lax.rsqrt(jnp.mean(saved * saved, axis=-1, keepdims=True) + 1e-06)
+    input_gradient, part = norm_reverse_pass(
+        outgrad_ref[rows_of(mp), :], normed_grad, saved * rstd, rstd, gain_ref[...]
+    )
+    gi_buf[...] = input_gradient.astype(BF16)
+    gain_slots[mp] = jnp.broadcast_to(part[None, :], gain_slots.shape[1:])
+    gi_keep.start()
+    for i in others:
+        gi_copy(i).start()
+        slot_copy(i).start()
+
     def count(array):
         return pieces if array < 3 else per_chunk
 
@@ -394,6 +513,15 @@
             return carry
 
         lax.fori_loop(0, count(array), pass_on, 0)
+        if array == 0:
+            for i in others:
+                slot_copy(i).wait()
+            part = gain_slots[0]
+            for i in others:
+                part += gain_slots[i]
+            gain_seqs[me] = part.astype(BF16).astype(F32)
+            for mask in (1, 2, 3):
+                seq_copy(mask).start()
     for array in range(4):
 
         def finish(piece, carry, array=array):
@@ -404,70 +532,17 @@
             return carry
 
         lax.fori_loop(0, count(array), finish, 0)
-
-
-def fused_grads(
-    normalized_rows, query_saved, key_saved, value_saved, w_query, w_key, w_value, w_out, output_gradient
-):
-    length, width = query_saved.shape
-    features = normalized_rows.shape[1]
-    steps = width // HD
-    per_chunk = steps // N_DP
-    rows = jnp.stack([normalized_rows.T, output_gradient.T])
-    vmem, hbm = pl.BlockSpec(memory_space=pltpu.VMEM), pl.BlockSpec(memory_space=pl.ANY)
-    dma = pltpu.SemaphoreType.DMA
-    grads, att, gathered, total = pl.pallas_call(
-        attention_kernel,
-        out_shape=(
-            jax.ShapeDtypeStruct((per_chunk, N_DP, length, 3 * HD), BF16),
-            jax.ShapeDtypeStruct((per_chunk, N_DP, HD, length), BF16),
-            jax.ShapeDtypeStruct((2, N_DP, features, length), BF16),
-            jax.ShapeDtypeStruct((length, features), BF16),
-        ),
-        in_specs=[vmem] * 8,
-        out_specs=(hbm, hbm, hbm, vmem),
-        scratch_shapes=[
-            pltpu.VMEM((steps, length, 3 * HD), BF16),
-            pltpu.VMEM((steps, HD, length), BF16),
-            pltpu.VMEM((length, features), F32),
-            dma((2, steps)),
-            dma((2, steps)),
-            dma((12,)),
-            dma((12,)),
-            dma((2,)),
-        ],
-        compiler_params=pltpu.CompilerParams(
-            collective_id=0, has_side_effects=True, vmem_limit_bytes=56 * 2**20
-        ),
-        cost_estimate=pl.CostEstimate(
-            flops=30 * length * width * features, bytes_accessed=40 * 2**20, transcendentals=0
-        ),
-    )(query_saved, key_saved, value_saved, w_query, w_key, w_value, w_out, rows)
-    pieces = 4
-    outs = pl.pallas_call(
-        weight_kernel,
-        out_shape=(jax.ShapeDtypeStruct((features, width), BF16),) * 3
-        + (jax.ShapeDtypeStruct((width, features), BF16),),
-        in_specs=[vmem] * 3,
-        out_specs=(hbm,) * 4,
-        scratch_shapes=[
-            pltpu.VMEM((3, pieces, features // pieces, per_chunk * HD), BF16),
-            pltpu.VMEM((per_chunk, HD, features), BF16),
-            dma((4, 4, max(pieces, per_chunk))),
-            dma((4, 4, max(pieces, per_chunk))),
-            dma((4, max(pieces, per_chunk))),
-        ],
-        compiler_params=pltpu.CompilerParams(
-            collective_id=1, has_side_effects=True, vmem_limit_bytes=48 * 2**20
-        ),
-        cost_estimate=pl.CostEstimate(
-            flops=200 * length * width * features, bytes_accessed=200 * 2**20, transcendentals=0
-        ),
-    )(grads, att, gathered)
-    return total, outs
+    for mask in (1, 2, 3):
+        seq_copy(mask).wait()
+    gain_out[...] = (gain_seqs[0] + gain_seqs[1]) + (gain_seqs[2] + gain_seqs[3])
+    for i in others:
+        total_copy(i).wait_send()
+        gi_copy(i).wait()
+    gi_keep.wait()
 
 
 def fused_shards(
+    n_mp,
     inputs,
     norm_gain_vector,
     query_saved,
@@ -483,22 +558,81 @@
     reciprocal_deviation = lax.rsqrt(
         jnp.mean(widened_rows * widened_rows, axis=-1, keepdims=True) + 1e-06
     )
-    unit_input_rows = widened_rows * reciprocal_deviation
-    normalized_rows = (unit_input_rows * norm_gain_vector).astype(BF16)
-    total, outs = fused_grads(
-        normalized_rows, query_saved, key_saved, value_saved, w_query, w_key, w_value, w_out,
-        output_gradient,
-    )
-    normalized_gradient = lax.psum(total, "mp").astype(F32)
-    input_gradient, partial_gain = norm_reverse_pass(
-        output_gradient,
-        normalized_gradient,
-        unit_input_rows,
-        reciprocal_deviation,
-        norm_gain_vector,
-    )
-    sum_gain = lax.psum(partial_gain.astype(BF16), "dp").astype(F32)
-    return (input_gradient.astype(BF16), *outs, sum_gain)
+    normalized_rows = (widened_rows * reciprocal_deviation * norm_gain_vector).astype(BF16)
+    length, width = query_saved.shape
+    features = normalized_rows.shape[1]
+    steps = width // HD
+    per_chunk = steps // N_DP
+    rows = jnp.stack([normalized_rows.T, output_gradient.T])
+    vmem, hbm = pl.BlockSpec(memory_space=pltpu.VMEM), pl.BlockSpec(memory_space=pl.ANY)
+    dma = pltpu.SemaphoreType.DMA
+    grads, att, gathered, total = pl.pallas_call(
+        functools.partial(attention_kernel, n_mp),
+        out_shape=(
+            jax.ShapeDtypeStruct((per_chunk, N_DP, length, 3 * HD), BF16),
+            jax.ShapeDtypeStruct((per_chunk, N_DP, HD, length), BF16),
+            jax.ShapeDtypeStruct((2, N_DP, features, length), BF16),
+            jax.ShapeDtypeStruct((length, features), BF16),
+        ),
+        in_specs=[hbm] * 7 + [vmem],
+        out_specs=(hbm, hbm, hbm, vmem),
+        scratch_shapes=[pltpu.VMEM((length, width), BF16)] * 3
+        + [pltpu.VMEM((features, width), BF16)] * 3
+        + [pltpu.VMEM((width, features), BF16)]
+        + [
+            pltpu.VMEM((steps, length, 3 * HD), BF16),
+            pltpu.VMEM((steps, HD, length), BF16),
+            pltpu.VMEM((length, features), F32),
+            dma((2, steps)),
+            dma((2, steps)),
+            dma((3 * n_mp,)),
+            dma((3 * n_mp,)),
+            dma((2,)),
+            dma((7,)),
+        ],
+        compiler_params=pltpu.CompilerParams(
+            collective_id=0, has_side_effects=True, vmem_limit_bytes=56 * 2**20
+        ),
+        cost_estimate=pl.CostEstimate(
+            flops=30 * length * width * features, bytes_accessed=40 * 2**20, transcendentals=0
+        ),
+    )(query_saved, key_saved, value_saved, w_query, w_key, w_value, w_out, rows)
+    pieces = 4
+    outs = pl.pallas_call(
+        functools.partial(weight_kernel, n_mp),
+        out_shape=(jax.ShapeDtypeStruct((features, width), BF16),) * 3
+        + (
+            jax.ShapeDtypeStruct((width, features), BF16),
+            jax.ShapeDtypeStruct((length, features), BF16),
+            jax.ShapeDtypeStruct((8, features), F32),
+        ),
+        in_specs=[vmem, hbm, hbm, vmem, vmem, vmem, vmem],
+        out_specs=(hbm,) * 5 + (vmem,),
+        scratch_shapes=[
+            pltpu.VMEM(att.shape, BF16),
+            pltpu.VMEM(gathered.shape, BF16),
+            pltpu.VMEM((3, pieces, features // pieces, per_chunk * HD), BF16),
+            pltpu.VMEM((per_chunk, HD, features), BF16),
+            pltpu.VMEM((n_mp, length // n_mp, features), BF16),
+            pltpu.VMEM((length // n_mp, features), BF16),
+            pltpu.VMEM((n_mp, 8, features), F32),
+            pltpu.VMEM((N_DP, 8, features), F32),
+            dma((4, 4, max(pieces, per_chunk))),
+            dma((4, 4, max(pieces, per_chunk))),
+            dma((4, max(pieces, per_chunk))),
+            dma((3,)),
+        ]
+        + [dma((n_mp,))] * 6
+        + [dma((N_DP,))] * 2,
+        compiler_params=pltpu.CompilerParams(
+            collective_id=1, has_side_effects=True, vmem_limit_bytes=48 * 2**20
+        ),
+        cost_estimate=pl.CostEstimate(
+            flops=200 * length * width * features, bytes_accessed=200 * 2**20, transcendentals=0
+        ),
+    )(grads, att, gathered, total, inputs, output_gradient, norm_gain_vector.reshape(1, features))
+    *weights, grad_inputs, sum_gain = outs
+    return (grad_inputs, *weights, sum_gain[0])
 
 
 def fits(mesh, arguments):
@@ -506,7 +640,7 @@
     n_dp, n_mp = mesh.shape["dp"], mesh.shape["mp"]
     return (
         n_dp == N_DP
-        and n_mp % 4 == 0
+        and n_mp == 8
         and width % (n_mp * N_DP * HD) == 0
         and width <= 2048 * n_mp
         and length == 512 * n_dp
@@ -517,7 +651,7 @@
 def solution(mesh):
     def whole(*arguments):
         return jax.shard_map(
-            fused_shards if fits(mesh, arguments) else shards,
+            functools.partial(fused_shards, mesh.shape["mp"]) if fits(mesh, arguments) else shards,
             mesh=mesh,
             in_specs=(
                 P("dp", None),

time: 324 us -> 281 us (0.87)
  Pallas kernels: 272 us -> 258 us
  between operations: 14.2 us -> 0.71 us
  blocking collectives: 8.9 us -> 0 us
  other arithmetic: 6.58 us -> 2.08 us
    pallas_call x2, Pallas kernels: 272 us -> 258 us  [the longest x1 145 us: fused_shards(): pl.pallas_call(functools.partial(weight_kernel, n_mp), out_shape=(jax.Sha...]
    psum x1 -> x0, blocking collectives: 8.9 us -> none  [fused_shards(): sum_gain = lax.psum(partial_gain.astype(BF16), 'dp').astype(F32)]
    unnamed x35 -> x21, local copies, waits for them, and re-layouts: 18.8 us -> 19.2 us
  transfers between devices with their start and end apart: 1 -> 0, of which waited for: 0 -> 0; matrix products, arithmetic and copies ran while one was open for 0% -> 0% of each run, Pallas kernels for 44% -> 0%
where the time goes in v2:
time: 281 us; the launch traced here: 280 us
  Pallas kernels  258 us (92%)
  local copies, waits for them, and re-layouts  19.8 us (7%)
    pallas_call x1, Pallas kernels, fused_shards(): pl.pallas_call(functools.partial(weight_kernel, n_mp), out_shape=(jax.Sha...  145 us
    pallas_call x1, Pallas kernels, fused_shards(): pl.pallas_call(functools.partial(attention_kernel, n_mp), out_shape=(jax....  113 us
    unnamed x21, local copies, waits for them, and re-layouts  19.2 us

profile of v2, /device:TPU:0, one launch (start us, length us, event | category | flops | bytes accessed | tf_op | source)
XLA Modules:
  0.0 280.4 jit_solution(18096856394059461784)
XLA Ops:
  0.6 0.0 copy-start.2
  0.6 1.5 copy.16
  2.1 0.0 copy-start
  2.2 0.3 fusion
  2.4 0.0 copy-done.2
  2.4 0.3 fusion.3
  2.8 0.6 copy-done
  3.4 0.5 copy.17
  3.9 1.5 pad_maximum_fusion.rows_ref
  5.4 0.0 copy-start.1
  5.4 113.1 %shard_map.145 = (bf16[4,4,512,384]{3,2,1,0:T(8,128)(2,1)}, bf16[4,4,128,512]{3,2,1,0:T(8,128)(2,1)}, bf16[2,4,1024,512]{3,2,1,0:T(8,128)(2,1)}, bf16[512,1024]{1,0:T(8,128)(2,1)}) custom-call(bf16[512,2048]{1,0:T(8,128)(2,1)} %q_hbm.1, bf16[512,2048]{1,0:T(8,128)(2,1)} %k_hbm.1, bf16[512,2048]{1,0:T(8,128)(2,1)} %v_hbm.1, bf16[1024,2048]{1,0:T(8,128)(2,1)} %wq_hbm.1, ...), custom_call_target="tpu_custom_call" | custom-call | flops 32212254720 | bytes 41943040 | tf_op jit(solution)/shard_map/pallas_call | solution.py:569
  118.6 0.0 copy-done.1
  118.6 0.0 copy-start.3
  118.6 1.2 copy-done.3
  119.8 144.7 %shard_map.146 = (bf16[1024,2048]{1,0:T(8,128)(2,1)}, bf16[1024,2048]{1,0:T(8,128)(2,1)}, bf16[1024,2048]{1,0:T(8,128)(2,1)}, bf16[2048,1024]{1,0:T(8,128)(2,1)}...) custom-call(bf16[4,4,512,384]{3,2,1,0:T(8,128)(2,1)} %get-tuple-element.16.grads_ref, ...), custom_call_target="tpu_custom_call" | custom-call | flops 214748364800 | bytes 209715200 | tf_op jit(solution)/shard_map/pallas_call | solution.py:601
  264.5 0.6 slice.3
  265.1 1.0 copy.23
  266.1 0.0 copy-start.6
  266.1 4.9 %copy.24 = bf16[1024,2048]{1,0:T(8,128)(2,1)} copy(bf16[1024,2048]{1,0:T(8,128)(2,1)} %get-tuple-element.33) | data formatting | bytes 8388608
  271.0 0.0 copy-done.6
  271.0 0.0 copy-start.5
  271.0 2.1 copy.25
  273.1 1.6 copy-done.5
  274.7 0.0 copy-start.4
  274.7 2.1 copy.26
  276.8 1.6 copy-done.4
  278.4 2.0 copy.27
  (1 shorter events, 0.0 us)
Async XLA Ops:
  0.6 1.8 copy-start.2
  2.1 1.2 copy-start
  5.4 113.1 %copy-start.1 = (bf16[512,1024]{1,0:T(8,128)(2,1)S(1)}, bf16[512,1024]{1,0:T(8,128)(2,1)}, u32[]{:S(2)}) copy-start(bf16[512,1024]{1,0:T(8,128)(2,1)} %inputs_ref.1) | copy-start | bytes 3145732
  118.6 1.2 copy-start.3
  266.1 4.9 %copy-start.6 = (bf16[1024,2048]{1,0:T(8,128)(2,1)S(1)}, bf16[1024,2048]{1,0:T(8,128)(2,1)}, u32[]{:S(2)}) copy-start(bf16[1024,2048]{1,0:T(8,128)(2,1)} %get-tuple-element.34) | copy-start | bytes 12582916
  271.0 3.7 %copy-start.5 = (bf16[1024,2048]{1,0:T(8,128)(2,1)S(1)}, bf16[1024,2048]{1,0:T(8,128)(2,1)}, u32[]{:S(2)}) copy-start(bf16[1024,2048]{1,0:T(8,128)(2,1)} %get-tuple-element.35) | copy-start | bytes 12582916
  274.7 3.7 %copy-start.4 = (bf16[2048,1024]{1,0:T(8,128)(2,1)S(1)}, bf16[2048,1024]{1,0:T(8,128)(2,1)}, u32[]{:S(2)}) copy-start(bf16[2048,1024]{1,0:T(8,128)(2,1)} %get-tuple-element.36) | copy-start | bytes 12582916

commit v3 on v2

--- a/solution.py
+++ b/solution.py
@@ -156,13 +156,17 @@
     pl.semaphore_wait(barrier, len(partners))
 
 
-def attention_kernel(
+def fused_kernel(
     n_mp,
-    q_hbm, k_hbm, v_hbm, wq_hbm, wk_hbm, wv_hbm, wo_hbm, rows_ref,
-    grads_out, att_out, gathered_out, total_out,
+    q_hbm, k_hbm, v_hbm, wq_hbm, wk_hbm, wv_hbm, wo_hbm,
+    rows_ref, inputs_ref, outgrad_ref, gain_ref,
+    gathered_out, gq_out, gk_out, gv_out, go_out, gi_out, gain_out,
     q_ref, k_ref, v_ref, wq_ref, wk_ref, wv_ref, wo_ref,
-    grads_buf, att_buf, total,
-    a2a_send, a2a_recv, gather_send, gather_recv, local_sem, load_sem,
+    grads_buf, att_buf, total, total_ref, grads_ref, att_ref,
+    landing, gi_buf, gain_slots, gain_seqs,
+    a2a_send, a2a_recv, gather_send, gather_recv, local_sem, load_sem, unpack_sem,
+    send_sem, recv_sem, keep_sem,
+    total_send, total_recv, gi_send, gi_recv, slot_send, slot_recv, seq_send, seq_recv,
 ):
     me, mp = lax.axis_index("dp"), lax.axis_index("mp")
     parts = n_mp // 2
@@ -185,8 +189,7 @@
 
     greet(
         [(flipped(me, mask), mp) for mask in (1, 2, 3)]
-        + [other_core]
-        + [along(j) for j in range(1, parts)]
+        + [(me, (mp + i) % n_mp) for i in range(1, n_mp)]
     )
     depth = rows_ref.shape[1] // parts
     steps = grads_buf.shape[0]
@@ -229,7 +232,7 @@
     def place(step):
         return step // N_DP, flipped(me, (step % N_DP + 1) % N_DP)
 
-    def remote(step):
+    def remote(step, kinds=(0, 1)):
         k, target = place(step)
         return [
             pltpu.make_async_remote_copy(
@@ -240,14 +243,16 @@
                 device_id=(target, mp),
                 device_id_type=MESH,
             )
-            for i, (buf, out) in enumerate(((grads_buf, grads_out), (att_buf, att_out)))
+            for i, (buf, out) in enumerate(((grads_buf, grads_ref), (att_buf, att_ref)))
+            if i in kinds
         ]
 
-    def local(step):
+    def local(step, kinds=(0, 1)):
         k, _ = place(step)
         return [
             pltpu.make_async_copy(buf.at[step], out.at[k, me], a2a_send.at[i, step])
-            for i, (buf, out) in enumerate(((grads_buf, grads_out), (att_buf, att_out)))
+            for i, (buf, out) in enumerate(((grads_buf, grads_ref), (att_buf, att_ref)))
+            if i in kinds
         ]
 
     total[...] = jnp.zeros_like(total)
@@ -300,60 +305,11 @@
             along_z(mask, j).start()
         across(mask, 0).start()
     lax.fori_loop(N_DP, steps, head_step, 0)
-    total_out[...] = total[...].astype(BF16)
-    for j in range(1, parts):
-        for mask in (1, 2, 3):
-            along_z(mask, j).wait_recv()
-            across(mask, j).start()
-
-    def drain(step, carry):
-        @pl.when(step % N_DP != N_DP - 1)
-        def _():
-            for copy in remote(step):
-                copy.wait()
-
-        @pl.when(step % N_DP == N_DP - 1)
-        def _():
-            for copy in local(step):
-                copy.wait()
-
-        return carry
-
-    lax.fori_loop(0, steps, drain, 0)
-    for mask in (1, 2, 3):
-        spread(mask).wait_send()
-        for j in range(1, parts):
-            along_z(mask, j).wait_send()
-        for j in range(parts):
-            across(mask, j).wait()
-    own_rows(0).wait()
-    own_rows(1).wait()
-
-
-def weight_kernel(
-    n_mp,
-    grads_ref, att_hbm, gathered_hbm, total_ref, inputs_ref, outgrad_ref, gain_ref,
-    gq_out, gk_out, gv_out, go_out, gi_out, gain_out,
-    att_ref, gathered_ref, wide, tall, landing, gi_buf, gain_slots, gain_seqs,
-    send_sem, recv_sem, local_sem, load_sem,
-    total_send, total_recv, gi_send, gi_recv, slot_send, slot_recv, seq_send, seq_recv,
-):
-    me, mp = lax.axis_index("dp"), lax.axis_index("mp")
-    peer_x, peer_y = flipped(me, 1), flipped(me, 2)
-    loads = [
-        pltpu.make_async_copy(gathered_hbm.at[0], gathered_ref.at[0], load_sem.at[0]),
-        pltpu.make_async_copy(att_hbm, att_ref, load_sem.at[1]),
-        pltpu.make_async_copy(gathered_hbm.at[1], gathered_ref.at[1], load_sem.at[2]),
-    ]
-    for load in loads:
-        load.start()
+    total_ref[...] = total[...].astype(BF16)
 
     def ahead(i):
         return (mp + i) % n_mp
 
-    greet(
-        [(flipped(me, mask), mp) for mask in (1, 2, 3)] + [(me, ahead(i)) for i in range(1, n_mp)]
-    )
     share = total_ref.shape[0] // n_mp
 
     def rows_of(index):
@@ -403,9 +359,31 @@
     others = range(1, n_mp)
     for i in others:
         total_copy(i).start()
-    per_chunk = grads_ref.shape[0]
-    pieces = wide.shape[1]
-    height, width = wide.shape[2], wide.shape[3]
+    for j in range(1, parts):
+        for mask in (1, 2, 3):
+            along_z(mask, j).wait_recv()
+            across(mask, j).start()
+    own_rows(0).wait()
+    own_rows(1).wait()
+    for j in range(parts):
+        for mask in (1, 2, 3):
+            across(mask, j).wait_recv()
+    length = rows_ref.shape[2]
+    unpacks = [
+        pltpu.make_async_copy(
+            gathered_out.at[array, owner],
+            ref.at[:, owner * length : (owner + 1) * length],
+            unpack_sem.at[array, owner],
+        )
+        for array, ref in ((1, wk_ref), (0, wq_ref))
+        for owner in range(N_DP)
+    ]
+    for unpack in unpacks:
+        unpack.start()
+
+    peer_x, peer_y = flipped(me, 1), flipped(me, 2)
+    pieces = 4
+    height, width = rows_ref.shape[1] // pieces, per_chunk * HD
     outs = (gq_out, gk_out, gv_out, go_out)
 
     def spot(array, piece, owner, part=None):
@@ -421,7 +399,12 @@
         return outs[array].at[pl.ds(pl.multiple_of(first, size), size), cols]
 
     def staged(array, piece):
-        return wide.at[array, piece] if array < 3 else tall.at[piece]
+        if array == 3:
+            return wo_ref.at[pl.ds(pl.multiple_of(piece * HD, HD), HD)]
+        across_rows = q_ref.shape[0] // height
+        rows = pl.ds(pl.multiple_of(piece % across_rows * height, height), height)
+        cols = pl.ds(pl.multiple_of(piece // across_rows * width, width), width)
+        return (q_ref, k_ref, v_ref)[array].at[rows, cols]
 
     def copy_to(kind, array, piece, src, dst, peer):
         return pltpu.make_async_remote_copy(
@@ -444,7 +427,7 @@
 
     def keep(array, piece):
         return pltpu.make_async_copy(
-            staged(array, piece), spot(array, piece, me), local_sem.at[array, piece]
+            staged(array, piece), spot(array, piece, me), keep_sem.at[array, piece]
         )
 
     def send(array, piece):
@@ -452,7 +435,40 @@
         own(1, array, piece).start()
         keep(array, piece).start()
 
-    loads[0].wait()
+    def settle(step, i):
+        @pl.when(step % N_DP != N_DP - 1)
+        def _():
+            remote(step, (i,))[0].wait_recv()
+
+        @pl.when(step % N_DP == N_DP - 1)
+        def _():
+            local(step, (i,))[0].wait()
+
+    def settle_step(i, step, carry):
+        settle(step, i)
+        return carry
+
+    for unpack in unpacks[:N_DP]:
+        unpack.wait()
+
+    def tall_step(piece, carry):
+        lax.fori_loop(
+            piece * N_DP, (piece + 1) * N_DP, functools.partial(settle_step, 1), 0
+        )
+        acc = None
+        for owner in range(N_DP):
+            term = dot_nt(
+                att_ref[piece, owner], wk_ref[:, owner * length : (owner + 1) * length]
+            )
+            acc = term if acc is None else acc + term
+        staged(3, piece)[...] = acc.astype(BF16)
+        send(3, piece)
+        return carry
+
+    lax.fori_loop(0, per_chunk, tall_step, 0)
+    for unpack in unpacks[N_DP:]:
+        unpack.wait()
+    lax.fori_loop(0, steps, functools.partial(settle_step, 0), 0)
     for array in range(3):
         lanes = slice(array * HD, (array + 1) * HD)
 
@@ -463,27 +479,13 @@
                 right = jnp.concatenate(
                     [grads_ref[k, owner, :, lanes] for k in range(per_chunk)], axis=1
                 )
-                term = dot_nn(gathered_ref[0, owner, rows, :], right)
+                term = dot_nn(wq_ref[rows, owner * length : (owner + 1) * length], right)
                 acc = term if acc is None else acc + term
-            wide[array, piece] = acc.astype(BF16)
+            staged(array, piece)[...] = acc.astype(BF16)
             send(array, piece)
             return carry
 
         lax.fori_loop(0, pieces, wide_step, 0)
-
-    loads[1].wait()
-    loads[2].wait()
-
-    def tall_step(piece, carry):
-        acc = None
-        for owner in range(N_DP):
-            term = dot_nt(att_ref[piece, owner], gathered_ref[1, owner])
-            acc = term if acc is None else acc + term
-        tall[piece] = acc.astype(BF16)
-        send(3, piece)
-        return carry
-
-    lax.fori_loop(0, per_chunk, tall_step, 0)
 
     normed_grad = total_ref[rows_of(mp), :].astype(F32)
     for i in others:
@@ -504,7 +506,7 @@
     def count(array):
         return pieces if array < 3 else per_chunk
 
-    for array in range(4):
+    for array in (3, 0, 1, 2):
 
         def pass_on(piece, carry, array=array):
             for kind in (0, 1):
@@ -513,7 +515,7 @@
             return carry
 
         lax.fori_loop(0, count(array), pass_on, 0)
-        if array == 0:
+        if array == 3:
             for i in others:
                 slot_copy(i).wait()
             part = gain_slots[0]
@@ -539,6 +541,59 @@
         total_copy(i).wait_send()
         gi_copy(i).wait()
     gi_keep.wait()
+
+    def drain(step, carry):
+        @pl.when(step % N_DP != N_DP - 1)
+        def _():
+            for copy in remote(step):
+                copy.wait_send()
+
+        return carry
+
+    lax.fori_loop(0, steps, drain, 0)
+    for mask in (1, 2, 3):
+        spread(mask).wait_send()
+        for j in range(1, parts):
+            along_z(mask, j).wait_send()
+        for j in range(parts):
+            across(mask, j).wait_send()
+
+
+def place_kernel(count, *refs):
+    sources, targets, stages = refs[:count], refs[count : 2 * count], refs[2 * count : 3 * count]
+    read_sem, write_sem = refs[3 * count :]
+
+    def copies(array, part):
+        rows = sources[array].shape[0] // 4
+        block = pl.ds(part * rows, rows)
+        stage = stages[array].at[block]
+        return (
+            pltpu.make_async_copy(sources[array].at[block], stage, read_sem.at[array, part]),
+            pltpu.make_async_copy(stage, targets[array].at[block], write_sem.at[array, part]),
+        )
+
+    pairs = [copies(array, part) for array in range(count) for part in range(4)]
+    for read, _ in pairs:
+        read.start()
+    for read, write in pairs:
+        read.wait()
+        write.start()
+    for _, write in pairs:
+        write.wait()
+
+
+def placed(arrays):
+    hbm = pl.BlockSpec(memory_space=pl.ANY)
+    count = len(arrays)
+    return pl.pallas_call(
+        functools.partial(place_kernel, count),
+        out_shape=tuple(jax.ShapeDtypeStruct(a.shape, a.dtype) for a in arrays),
+        in_specs=[hbm] * count,
+        out_specs=(hbm,) * count,
+        scratch_shapes=[pltpu.VMEM(a.shape, a.dtype) for a in arrays]
+        + [pltpu.SemaphoreType.DMA((count, 4))] * 2,
+        compiler_params=pltpu.CompilerParams(vmem_limit_bytes=60 * 2**20),
+    )(*arrays)
 
 
 def fused_shards(
@@ -566,16 +621,18 @@
     rows = jnp.stack([normalized_rows.T, output_gradient.T])
     vmem, hbm = pl.BlockSpec(memory_space=pltpu.VMEM), pl.BlockSpec(memory_space=pl.ANY)
     dma = pltpu.SemaphoreType.DMA
-    grads, att, gathered, total = pl.pallas_call(
-        functools.partial(attention_kernel, n_mp),
-        out_shape=(
-            jax.ShapeDtypeStruct((per_chunk, N_DP, length, 3 * HD), BF16),
-            jax.ShapeDtypeStruct((per_chunk, N_DP, HD, length), BF16),
-            jax.ShapeDtypeStruct((2, N_DP, features, length), BF16),
+    pieces = max(4, per_chunk)
+    _, *weights, grad_inputs, sum_gain = pl.pallas_call(
+        functools.partial(fused_kernel, n_mp),
+        out_shape=(jax.ShapeDtypeStruct((2, N_DP, features, length), BF16),)
+        + (jax.ShapeDtypeStruct((features, width), BF16),) * 3
+        + (
+            jax.ShapeDtypeStruct((width, features), BF16),
             jax.ShapeDtypeStruct((length, features), BF16),
+            jax.ShapeDtypeStruct((8, features), F32),
         ),
-        in_specs=[hbm] * 7 + [vmem],
-        out_specs=(hbm, hbm, hbm, vmem),
+        in_specs=[hbm] * 7 + [vmem] * 4,
+        out_specs=(hbm,) * 6 + (vmem,),
         scratch_shapes=[pltpu.VMEM((length, width), BF16)] * 3
         + [pltpu.VMEM((features, width), BF16)] * 3
         + [pltpu.VMEM((width, features), BF16)]
@@ -583,56 +640,37 @@
             pltpu.VMEM((steps, length, 3 * HD), BF16),
             pltpu.VMEM((steps, HD, length), BF16),
             pltpu.VMEM((length, features), F32),
+            pltpu.VMEM((length, features), BF16),
+            pltpu.VMEM((per_chunk, N_DP, length, 3 * HD), BF16),
+            pltpu.VMEM((per_chunk, N_DP, HD, length), BF16),
+            pltpu.VMEM((n_mp, length // n_mp, features), BF16),
+            pltpu.VMEM((length // n_mp, features), BF16),
+            pltpu.VMEM((n_mp, 8, features), F32),
+            pltpu.VMEM((N_DP, 8, features), F32),
             dma((2, steps)),
             dma((2, steps)),
             dma((3 * n_mp,)),
             dma((3 * n_mp,)),
             dma((2,)),
             dma((7,)),
-        ],
-        compiler_params=pltpu.CompilerParams(
-            collective_id=0, has_side_effects=True, vmem_limit_bytes=56 * 2**20
-        ),
-        cost_estimate=pl.CostEstimate(
-            flops=30 * length * width * features, bytes_accessed=40 * 2**20, transcendentals=0
-        ),
-    )(query_saved, key_saved, value_saved, w_query, w_key, w_value, w_out, rows)
-    pieces = 4
-    outs = pl.pallas_call(
-        functools.partial(weight_kernel, n_mp),
-        out_shape=(jax.ShapeDtypeStruct((features, width), BF16),) * 3
-        + (
-            jax.ShapeDtypeStruct((width, features), BF16),
-            jax.ShapeDtypeStruct((length, features), BF16),
-            jax.ShapeDtypeStruct((8, features), F32),
-        ),
-        in_specs=[vmem, hbm, hbm, vmem, vmem, vmem, vmem],
-        out_specs=(hbm,) * 5 + (vmem,),
-        scratch_shapes=[
-            pltpu.VMEM(att.shape, BF16),
-            pltpu.VMEM(gathered.shape, BF16),
-            pltpu.VMEM((3, pieces, features // pieces, per_chunk * HD), BF16),
-            pltpu.VMEM((per_chunk, HD, features), BF16),
-            pltpu.VMEM((n_mp, length // n_mp, features), BF16),
-            pltpu.VMEM((length // n_mp, features), BF16),
-            pltpu.VMEM((n_mp, 8, features), F32),
-            pltpu.VMEM((N_DP, 8, features), F32),
-            dma((4, 4, max(pieces, per_chunk))),
-            dma((4, 4, max(pieces, per_chunk))),
-            dma((4, max(pieces, per_chunk))),
-            dma((3,)),
+            dma((2, N_DP)),
+            dma((4, 4, pieces)),
+            dma((4, 4, pieces)),
+            dma((4, pieces)),
         ]
         + [dma((n_mp,))] * 6
         + [dma((N_DP,))] * 2,
         compiler_params=pltpu.CompilerParams(
-            collective_id=1, has_side_effects=True, vmem_limit_bytes=48 * 2**20
+            collective_id=0, has_side_effects=True, vmem_limit_bytes=60 * 2**20
         ),
         cost_estimate=pl.CostEstimate(
-            flops=200 * length * width * features, bytes_accessed=200 * 2**20, transcendentals=0
+            flops=46 * length * width * features, bytes_accessed=80 * 2**20, transcendentals=0
         ),
-    )(grads, att, gathered, total, inputs, output_gradient, norm_gain_vector.reshape(1, features))
-    *weights, grad_inputs, sum_gain = outs
-    return (grad_inputs, *weights, sum_gain[0])
+    )(
+        query_saved, key_saved, value_saved, w_query, w_key, w_value, w_out,
+        rows, inputs, output_gradient, norm_gain_vector.reshape(1, features),
+    )
+    return (*placed((grad_inputs, *weights)), sum_gain[0])
 
 
 def fits(mesh, arguments):
@@ -642,7 +680,7 @@
         n_dp == N_DP
         and n_mp == 8
         and width % (n_mp * N_DP * HD) == 0
-        and width <= 2048 * n_mp
+        and width == 2048 * n_mp
         and length == 512 * n_dp
         and arguments[0].shape[1] == 1024
     )

time: 281 us -> 272 us (0.968)
  local copies, waits for them, and re-layouts: 19.8 us -> 4.03 us
  Pallas kernels: 258 us -> 265 us
    unnamed x21 -> x6, local copies, waits for them, and re-layouts: 19.2 us -> 2.67 us
    pallas_call x2, Pallas kernels: 258 us -> 265 us  [the longest x1 252 us: fused_shards(): pl.pallas_call(functools.partial(fused_kernel, n_mp), out_shape=(jax.Shap...]
where the time goes in v3:
time: 272 us
  Pallas kernels  265 us (97%)
  local copies, waits for them, and re-layouts  4.03 us (1%)
    pallas_call x1, Pallas kernels, fused_shards(): pl.pallas_call(functools.partial(fused_kernel, n_mp), out_shape=(jax.Shap...  252 us
    pallas_call x1, Pallas kernels, placed(): pl.pallas_call(functools.partial(place_kernel, count), out_shape=tuple((j...  13.1 us

profile of v3, /device:TPU:0, one launch (start us, length us, event | category | flops | bytes accessed | tf_op | source)
XLA Modules:
  0.0 272.0 jit_solution(2946623146607185701)
XLA Ops:
  0.6 0.0 copy-start.1
  0.6 1.5 copy.16
  2.1 0.0 copy-start
  2.2 0.3 fusion
  2.4 0.0 copy-done.1
  2.5 0.3 fusion.3
  2.7 0.6 copy-done
  3.4 0.5 copy.17
  3.9 1.5 pad_maximum_fusion.rows_ref
  5.4 252.1 %shard_map.145 = (bf16[2,4,1024,512]{3,2,1,0:T(8,128)(2,1)}, bf16[1024,2048]{1,0:T(8,128)(2,1)}, bf16[1024,2048]{1,0:T(8,128)(2,1)}, bf16[1024,2048]{1,0:T(8,128...) custom-call(bf16[512,2048]{1,0:T(8,128)(2,1)} %q_hbm.1, ...), custom_call_target="tpu_custom_call" | custom-call | flops 49392123904 | bytes 83886080 | tf_op jit(solution)/shard_map/pallas_call | solution.py:625
  257.5 13.1 %shard_map.146 = (bf16[512,1024]{1,0:T(8,128)(2,1)}, bf16[1024,2048]{1,0:T(8,128)(2,1)}, bf16[1024,2048]{1,0:T(8,128)(2,1)}, bf16[1024,2048]{1,0:T(8,128)(2,1)}, bf16[2048,1024]{1,0:T(8,128)(2,1)}) custom-call(bf16[512,1024]{1,0:T(8,128)(2,1)} %get-tuple-element.17.refs_0_, bf16[1024,2048]{1,0:T(8,128)(2,1)} %get-tuple-element.18.refs_1_, ...), custom_call_target="tpu_custom_call" | custom-call | tf_op jit(solution)/shard_map/pallas_call | solution.py:588
  270.6 1.4 slice.3
  (1 shorter events, 0.0 us)
Async XLA Ops:
  0.6 1.8 copy-start.1
  2.1 1.2 copy-start
